TPU v7x, 512 devices: a whole 4x4x16 slice. The times are simulated.
512 devices in a mesh: hist: 64 (over z_lo, x, y), dom: 8 (over z_hi, core).
Axes of the slice: x: 4, y: 4, z: 16 (z_hi: 4, z_lo: 4; z = z_hi * 4 + z_lo), core: 2. Of those that a mesh axis runs over, the one named last changes fastest.
Arguments:
- coords: float32 [6, 1048576], P(None, ('dom', 'hist')), may hold values from -3 to 3
- charge: float32 [1048576], P(('dom', 'hist')), may hold values from 0.02 to 0.2
- row_index: int32 [1048576], P(('dom', 'hist')), may hold values from 0 to 511, as said below
- block_col: int32 [8192], P(('dom', 'hist')), may hold values from 0 to 496
- col_offset: int32 [1048576], P(('dom', 'hist')), may hold values from 0 to 15
- transfer_map: float32 [6, 84], replicated
- history: bfloat16 [512, 2, 512, 512], P('hist', None, 'dom'), may hold values from -16 to 16
- retard_index: int32 [512], P('hist'), may hold values from 0 to 16
- retard_frac: float32 [512], P('hist'), may hold values from 0 to 1
- retard_weight: float32 [512], P('hist'), may hold values from 0.005 to 0.05
- z_kernel: float32 [512, 512], P(None, 'dom')
- x_kernel: float32 [512, 512], replicated
Outputs:
- kicked: float32 [6, 1048576], P(None, ('dom', 'hist'))
- field: float32 [2, 512, 512], P(None, 'dom', 'hist')
- deposit: float32 [2, 512, 512], P(None, 'dom', 'hist')
Inputs may be any that keep to these rules, and one draw needn't show every extreme that they name: `row_index`: particle i lies in grid slab i // (1048576 // 8): its row is that slab's number times 64 plus 0 to 63.
All inputs are finite; a program needn't handle non-finite values.
Results may differ from a plain program's by a relative error of at most 0.0019.
Values may be sent and summed in bfloat16 or wider, within the bound.
A program may use at most 64 MiB of HBM per device.

v0:
```python
import jax
import jax.numpy as jnp
from jax import lax
from jax.sharding import PartitionSpec as P


def monomials(coords):
    products = [jnp.ones_like(coords[0])]
    for first in range(6):
        products.append(coords[first])
    for first in range(6):
        for second in range(first, 6):
            products.append(coords[first] * coords[second])
    for first in range(6):
        for second in range(first, 6):
            for third in range(second, 6):
                products.append(coords[first] * coords[second] * coords[third])
    return jnp.stack(products)


def retarded_source(history, retard_index, retard_frac, retard_weight):
    count_steps, comps, rows_here, width = history.shape

    def add_step(position, total):
        frame = lax.dynamic_index_in_dim(history, position, 0, keepdims=False).astype(jnp.float32)
        padded = jnp.pad(frame, ((0, 0), (0, 0), (width + 1, 0)))
        lag = retard_index[position]
        near = lax.dynamic_slice_in_dim(padded, width + 1 - lag, width, 2)
        far = lax.dynamic_slice_in_dim(padded, width - lag, width, 2)
        fraction = retard_frac[position]
        return total + retard_weight[position] * ((1.0 - fraction) * near + fraction * far)

    start = jnp.zeros((comps, rows_here, width), jnp.float32)
    return lax.fori_loop(0, count_steps, add_step, start)


def local(
    coords,
    charge,
    row_index,
    block_col,
    col_offset,
    transfer_map,
    history,
    retard_index,
    retard_frac,
    retard_weight,
    z_kernel,
    x_kernel,
):
    highest = lax.Precision.HIGHEST
    slab_rows = history.shape[2]
    width = history.shape[3]
    strip_width = width // lax.axis_size("hist")
    particles = coords.shape[1]
    group_size = min(1024, particles)
    count_groups = particles // group_size
    block_size = particles // block_col.shape[0]
    slab_start = lax.axis_index("dom") * slab_rows
    source = retarded_source(history, retard_index, retard_frac, retard_weight)
    spread = jnp.einsum("crx,xy->cry", source, x_kernel, precision=highest)
    partial_field = jnp.einsum("rs,csy->cry", z_kernel, spread, precision=highest)
    total_field = lax.psum(partial_field, ("hist", "dom"))
    slab_field = lax.dynamic_slice_in_dim(total_field, slab_start, slab_rows, 1)
    field_out = lax.dynamic_slice_in_dim(
        slab_field, lax.axis_index("hist") * strip_width, strip_width, 2
    )
    slab_rounded = slab_field.astype(jnp.bfloat16)
    folded = jnp.transpose(slab_rounded, (1, 0, 2)).reshape(slab_rows, 2 * width)
    pushed = jnp.dot(transfer_map, monomials(coords), precision=highest)
    column = jnp.repeat(block_col, block_size) + col_offset
    local_row = row_index - slab_start
    weight_pair = jnp.stack([charge, charge * pushed[1]]).astype(jnp.bfloat16)
    row_groups = local_row.reshape(count_groups, group_size)
    column_groups = column.reshape(count_groups, group_size)
    weight_groups = jnp.transpose(weight_pair.reshape(2, count_groups, group_size), (1, 0, 2))
    row_iota = lax.iota(jnp.int32, slab_rows)
    column_iota = lax.iota(jnp.int32, width)

    def one_group(accumulated, pieces):
        group_rows, group_columns, group_weights = pieces
        row_hot = (row_iota[:, None] == group_rows[None, :]).astype(jnp.bfloat16)
        column_hot = (group_columns[:, None] == column_iota[None, :]).astype(jnp.bfloat16)
        weighted = jnp.concatenate(
            [group_weights[0][:, None] * column_hot, group_weights[1][:, None] * column_hot], axis=1
        )
        accumulated = accumulated + jnp.dot(row_hot, weighted, preferred_element_type=jnp.float32)
        sampled_rows = lax.dot_general(
            row_hot, folded, (((0,), (0,)), ((), ())), preferred_element_type=jnp.float32
        )
        column_mask = column_hot.astype(jnp.float32)
        longitudinal = jnp.sum(sampled_rows[:, :width] * column_mask, axis=1)
        transverse = jnp.sum(sampled_rows[:, width:] * column_mask, axis=1)
        return (accumulated, jnp.stack([longitudinal, transverse]))

    empty = jnp.zeros((slab_rows, 2 * width), jnp.float32)
    deposit_local, sampled_groups = lax.scan(
        one_group, empty, (row_groups, column_groups, weight_groups)
    )
    sampled = jnp.transpose(sampled_groups, (1, 0, 2)).reshape(2, particles)
    deposit_split = lax.psum_scatter(
        deposit_local.reshape(slab_rows, 2, width), "hist", scatter_dimension=2, tiled=True
    )
    deposit_out = jnp.transpose(deposit_split, (1, 0, 2))
    kicked = pushed.at[5].add(0.5 * sampled[0]).at[1].add(0.5 * sampled[1])
    return (kicked, field_out, deposit_out)


def solution(mesh):
    return jax.shard_map(
        local,
        mesh=mesh,
        in_specs=(
            P(None, ("dom", "hist")),
            P(("dom", "hist")),
            P(("dom", "hist")),
            P(("dom", "hist")),
            P(("dom", "hist")),
            P(),
            P("hist", None, "dom", None),
            P("hist"),
            P("hist"),
            P("hist"),
            P(None, "dom"),
            P(),
        ),
        out_specs=(P(None, ("dom", "hist")), P(None, "dom", "hist"), P(None, "dom", "hist")),
        check_vma=False,
    )
```

profile of v0, /device:TPU:128, one launch (start us, length us, event | category | flops | bytes accessed | tf_op | source)
XLA Modules:
  0.0 956.1 jit_solution(17558240199381335158)
XLA Ops:
  7.2 76.3 %while.31 = (s32[]{:T(128)}, f32[2,64,512]{2,1,0:T(8,128)S(1)}, f32[8]{0:T(128)}, f32[8]{0:T(128)}, bf16[8,2,64,512]{3,2,1,0:T(8,128)(2,1)}, /*index=5*/s32[8]{0...) while((s32[]{:T(128)}, f32[2,64,512]{2,1,0:T(8,128)S(1)}, ...), condition=%wide.region_1.2_spmd.clone, body=%wide.region_0.1_spmd.clone.sunk | while | flops 524428 | bytes 1966899 | solution.py:34
  7.3 1.3 dynamic_slice.109
  8.6 1.3 dynamic_slice.108
  15.4 1.5 select_add_fusion.2
  18.1 1.3 dynamic_slice.108
  24.9 1.5 select_add_fusion.2
  27.6 1.3 dynamic_slice.108
  34.4 1.5 select_add_fusion.2
  37.2 1.3 dynamic_slice.108
  43.9 1.5 select_add_fusion.2
  45.4 1.2 dynamic_slice.109
  46.7 1.3 dynamic_slice.108
  53.5 1.5 select_add_fusion.2
  56.2 1.3 dynamic_slice.108
  63.0 1.5 select_add_fusion.2
  65.7 1.3 dynamic_slice.108
  72.5 1.5 select_add_fusion.2
  75.3 1.3 dynamic_slice.108
  82.0 1.5 select_add_fusion.2
  84.3 3.2 convolution_bitcast_fusion
  90.0 472.6 %all-reduce.3.cloned.1.call-done = f32[2,512,512]{1,2,0:T(8,128)} async-done(((f32[2,512,512]{1,2,0:T(8,128)}), f32[2,512,512]{1,2,0:T(8,128)}) %all-reduce.3.cloned.1.call-update) | async-done | bytes 2097168 | tf_op jit(solution)/shard_map/psum | solution.py:63
  564.0 5.3 while.32
  570.8 1.5 constant_dynamic-slice_fusion.2
  572.3 377.0 %reduce-scatter.2.cloned.1.call-done = f32[64,2,8]{0,2,1:T(8,128)} async-done(((f32[64,2,512]{0,2,1:T(8,128)}), f32[64,2,8]{0,2,1:T(8,128)}) %reduce-scatter.2.cloned.1.call-update) | async-done | bytes 4112 | tf_op jit(solution)/shard_map/reduce_scatter | solution.py:101
  (98 shorter events, 36.8 us)
Async XLA Ops:
  7.2 76.4 %copy-start = (f32[512,512]{1,0:T(8,128)S(1)}, f32[512,512]{1,0:T(8,128)}, u32[]{:S(2)}) copy-start(f32[512,512]{1,0:T(8,128)} %param.31) | copy-start | bytes 3145732
  7.2 555.5 %all-reduce.3.cloned.1.call-start = ((), (), s32[]{:S(2)}) async-start(), calls=%async_computation.1 | async-start | bytes 4194304 | tf_op jit(solution)/shard_map/psum | solution.py:63
  7.2 77.0 %copy-start.2 = (f32[512,64]{0,1:T(8,128)S(1)}, f32[512,64]{0,1:T(8,128)}, u32[]{:S(2)}) copy-start(f32[512,64]{0,1:T(8,128)} %param.30) | copy-start | bytes 393220
  84.3 3.3 copy-start.1
  84.3 3.5 copy-start.5
  84.3 3.5 copy-start.8
  87.5 0.7 copy-start.6
  87.5 1.9 copy-start.7
  87.5 2.4 copy-start.4
  87.5 861.8 %reduce-scatter.2.cloned.1.call-start = ((), (), s32[]{:S(2)}) async-start(), calls=%async_computation.2 | async-start | bytes 532480 | tf_op jit(solution)/shard_map/reduce_scatter | solution.py:101
  570.8 378.5 %copy-start.3 = (f32[6,2048]{1,0:T(8,128)}, f32[6,2048]{1,0:T(8,128)S(1)}, u32[]{:S(2)}) copy-start(f32[6,2048]{1,0:T(8,128)S(1)} %scatter-add.9) | copy-start | bytes 147460
Sparse Core Ops, SparseCore 0:
  87.6 474.9 all-reduce.2
  570.5 378.7 reduce-scatter.1
where the time goes:
time: 957 us; the launch traced here: 956 us
  waiting for transfers between devices  850 us (89%)
  local copies, waits for them, and re-layouts  43 us (4%)
  loops' own time  26.3 us (3%)
  other arithmetic  15.2 us (2%)
  between operations  14.3 us (1%)
    psum x1, waiting for transfers between devices, local(): total_field = lax.psum(partial_field, ('hist', 'dom'))  473 us
    reduce_scatter x1, waiting for transfers between devices, local(): lax.psum_scatter(deposit_local.reshape(slab_rows, 2, width), 'hist', scat...  377 us
    another operation x1, loops' own time, retarded_source(): return lax.fori_loop(0, count_steps, add_step, start)  26.2 us
  transfers between devices with their start and end apart: 2, of which 2 were waited for; matrix products, arithmetic and copies ran while one was open for 0% of the time, Pallas kernels for 0%

commit v1 on v0

--- a/solution.py
+++ b/solution.py
@@ -60,7 +60,7 @@
     source = retarded_source(history, retard_index, retard_frac, retard_weight)
     spread = jnp.einsum("crx,xy->cry", source, x_kernel, precision=highest)
     partial_field = jnp.einsum("rs,csy->cry", z_kernel, spread, precision=highest)
-    total_field = lax.psum(partial_field, ("hist", "dom"))
+    total_field = lax.psum(lax.psum(partial_field, "hist"), "dom")
     slab_field = lax.dynamic_slice_in_dim(total_field, slab_start, slab_rows, 1)
     field_out = lax.dynamic_slice_in_dim(
         slab_field, lax.axis_index("hist") * strip_width, strip_width, 2

time: 957 us -> 1350 us (1.41)
  waiting for transfers between devices: 850 us -> 1240 us
    psum x1 -> x2, waiting for transfers between devices: 473 us -> 860 us  [local(): total_field = lax.psum(lax.psum(partial_field, 'hist'), 'dom')]
  transfers between devices with their start and end apart: 2 -> 3, of which waited for: 2 -> 3; matrix products, arithmetic and copies ran while one was open for 0% -> 0% of each run, Pallas kernels for 0% -> 0%
where the time goes in v1:
time: 1350 us
  waiting for transfers between devices  1240 us (92%)
  local copies, waits for them, and re-layouts  42.9 us (3%)
  loops' own time  26.3 us (2%)
  other arithmetic  15.3 us (1%)
  between operations  14.1 us (1%)
    psum x2, waiting for transfers between devices, local(): total_field = lax.psum(lax.psum(partial_field, 'hist'), 'dom')  860 us
    reduce_scatter x1, waiting for transfers between devices, local(): lax.psum_scatter(deposit_local.reshape(slab_rows, 2, width), 'hist', scat...  379 us
  transfers between devices with their start and end apart: 3, of which 3 were waited for; matrix products, arithmetic and copies ran while one was open for 0% of the time, Pallas kernels for 0%

profile of v1, /device:TPU:128, one launch (start us, length us, event | category | flops | bytes accessed | tf_op | source)
XLA Modules:
  0.0 1345.3 jit_solution(13961173424506040685)
XLA Ops:
  7.2 76.3 %while.31 = (s32[]{:T(128)}, f32[2,64,512]{2,1,0:T(8,128)S(1)}, f32[8]{0:T(128)}, f32[8]{0:T(128)}, bf16[8,2,64,512]{3,2,1,0:T(8,128)(2,1)}, /*index=5*/s32[8]{0...) while((s32[]{:T(128)}, f32[2,64,512]{2,1,0:T(8,128)S(1)}, ...), condition=%wide.region_1.2_spmd.clone, body=%wide.region_0.1_spmd.clone.sunk | while | flops 524428 | bytes 1966899 | solution.py:34
  7.3 1.3 dynamic_slice.109
  8.6 1.3 dynamic_slice.108
  15.4 1.5 select_add_fusion.2
  18.1 1.3 dynamic_slice.108
  24.9 1.5 select_add_fusion.2
  27.6 1.3 dynamic_slice.108
  34.4 1.5 select_add_fusion.2
  37.2 1.3 dynamic_slice.108
  43.9 1.5 select_add_fusion.2
  46.7 1.3 dynamic_slice.108
  53.5 1.5 select_add_fusion.2
  56.2 1.3 dynamic_slice.108
  63.0 1.5 select_add_fusion.2
  65.7 1.3 dynamic_slice.108
  72.5 1.5 select_add_fusion.2
  75.3 1.3 dynamic_slice.108
  82.0 1.5 select_add_fusion.2
  84.3 3.2 convolution_bitcast_fusion
  87.8 729.1 %all-reduce.4.cloned.1.call-done = f32[2,512,512]{1,2,0:T(8,128)} async-done(((f32[2,512,512]{1,2,0:T(8,128)}), f32[2,512,512]{1,2,0:T(8,128)}) %all-reduce.4.cloned.1.call-update) | async-done | bytes 2097168 | tf_op jit(solution)/shard_map/psum | solution.py:63
  819.1 131.3 %all-reduce.6.cloned.1.call-done = f32[2,512,512]{1,2,0:T(8,128)} async-done(((f32[2,512,512]{1,2,0:T(8,128)}), f32[2,512,512]{1,2,0:T(8,128)}) %all-reduce.6.cloned.1.call-update) | async-done | bytes 2097168 | tf_op jit(solution)/shard_map/psum | solution.py:63
  951.7 5.3 while.32
  958.6 1.5 constant_dynamic-slice_fusion.2
  960.1 378.7 %reduce-scatter.2.cloned.1.call-done = f32[64,2,8]{0,2,1:T(8,128)} async-done(((f32[64,2,512]{0,2,1:T(8,128)}), f32[64,2,8]{0,2,1:T(8,128)}) %reduce-scatter.2.cloned.1.call-update) | async-done | bytes 4112 | tf_op jit(solution)/shard_map/reduce_scatter | solution.py:101
  (101 shorter events, 38.0 us)
Async XLA Ops:
  7.2 76.4 %copy-start = (f32[512,512]{1,0:T(8,128)S(1)}, f32[512,512]{1,0:T(8,128)}, u32[]{:S(2)}) copy-start(f32[512,512]{1,0:T(8,128)} %param.31) | copy-start | bytes 3145732
  7.2 809.8 %all-reduce.4.cloned.1.call-start = ((), (), s32[]{:S(2)}) async-start(), calls=%async_computation.1 | async-start | bytes 4194304 | tf_op jit(solution)/shard_map/psum | solution.py:63
  7.2 77.0 %copy-start.2 = (f32[512,64]{0,1:T(8,128)S(1)}, f32[512,64]{0,1:T(8,128)}, u32[]{:S(2)}) copy-start(f32[512,64]{0,1:T(8,128)} %param.30) | copy-start | bytes 393220
  84.3 3.3 copy-start.5
  84.3 3.3 copy-start.1
  87.5 729.6 %copy-start.6 = (s32[2048]{0:T(1024)S(1)}, s32[2048]{0:T(1024)}, u32[]{:S(2)}) copy-start(s32[2048]{0:T(1024)} %param.24) | copy-start | bytes 24580
  87.5 729.6 %copy-start.8 = (s32[16]{0:T(128)S(1)}, s32[16]{0:T(128)}, u32[]{:S(2)}) copy-start(s32[16]{0:T(128)} %param.23) | copy-start | bytes 196
  87.5 863.0 %all-reduce.6.cloned.1.call-start = ((), (), s32[]{:S(2)}) async-start(), calls=%async_computation.2 | async-start | bytes 4194304 | tf_op jit(solution)/shard_map/psum | solution.py:63
  817.0 1.5 copy-start.7
  817.0 2.0 copy-start.4
  817.0 521.8 %reduce-scatter.2.cloned.1.call-start = ((), (), s32[]{:S(2)}) async-start(), calls=%async_computation.3 | async-start | bytes 532480 | tf_op jit(solution)/shard_map/reduce_scatter | solution.py:101
  958.6 380.1 %copy-start.3 = (f32[6,2048]{1,0:T(8,128)}, f32[6,2048]{1,0:T(8,128)S(1)}, u32[]{:S(2)}) copy-start(f32[6,2048]{1,0:T(8,128)S(1)} %scatter-add.9) | copy-start | bytes 147460
Sparse Core Ops, SparseCore 0:
  87.6 729.3 all-reduce.3
  820.2 130.2 all-reduce.5
  958.3 380.4 reduce-scatter.1
